TPU v7x, 32 devices: a whole 2x2x4 slice. The times are simulated.
32 devices in a mesh: sec: 2 (over x), dp: 8 (over z, core), mp: 2 (over y).
Axes of the slice: x: 2, y: 2, z: 4, core: 2. Of those that a mesh axis runs over, the one named last changes fastest.
Arguments:
- queries: bfloat16 [64, 128, 4096], P(('sec', 'dp'), None, 'mp'), may hold values from -12 to 12
- keys_values: bfloat16 [256, 2, 32, 4096], P(('sec', 'dp'), None, None, 'mp'), may hold values from -5.5 to 5.5
- cotangent: bfloat16 [64, 128, 4096], P(('sec', 'dp'), None, 'mp'), may hold values from -4 to 4
- passage_slot: int32 [256], replicated, may hold values from 0 to 31, as said below
- passage_question: int32 [256], replicated, may hold values from 0 to 3, as said below
Outputs:
- grad_queries: bfloat16 [64, 128, 4096], P(('sec', 'dp'), None, 'mp')
- grad_keys_values: bfloat16 [256, 2, 32, 4096], P(('sec', 'dp'), None, None, 'mp')
- relevance: bfloat16 [256], P(('sec', 'dp'))
Inputs may be any that keep to these rules, and one draw needn't show every extreme that they name: A passage of section s goes to decoder device passage_slot // 4 of the other section, into its slot passage_slot % 4 for that encoder device. The passages of one device name distinct values, so one encoder device sends at most 4 passages to one decoder device, and every encoder device sends exactly 4 to some decoder device. `passage_question`: the question, among the 4 questions of its decoder device, that a passage serves; every question has at least one passage.
All inputs are finite; a program needn't handle non-finite values.
Results may differ from a plain program's by a relative error of at most 0.0014.
The roundings to bfloat16 on the way count: a program that leaves them out, or rounds other values in their place, can miss the bound.
Values may be sent and summed in bfloat16 or wider, within the bound.
A program may use at most 192 MiB of HBM per device.

v0:
```python
import math

import jax
import jax.numpy as jnp
from jax import lax
from jax.sharding import PartitionSpec as P

HEADS = 64
HD = 64
ANS = 128
SLOTS = 32


def partner(x, axis, distance):
    return lax.ppermute(x, axis, [(i, i ^ 1 << distance) for i in range(lax.axis_size(axis))])


def head_block(pieces, allowed, score_scale):
    query_part, key_part, value_part, grad_part = pieces
    scores = (
        jnp.einsum("rhc,khc->hrk", query_part, key_part, preferred_element_type=jnp.float32)
        * score_scale
    )
    scores = jnp.where(allowed[None], scores, -jnp.inf)
    row_max = jnp.max(scores, -1, keepdims=True)
    exponent = jnp.exp(scores - row_max)
    probability = exponent / jnp.sum(exponent, -1, keepdims=True)
    rounded_prob = probability.astype(jnp.bfloat16)
    attended = jnp.einsum(
        "hrk,khc->hrc", rounded_prob, value_part, preferred_element_type=jnp.float32
    )
    grad_prob = jnp.einsum(
        "rhc,khc->hrk", grad_part, value_part, preferred_element_type=jnp.float32
    )
    row_delta = jnp.sum(jnp.swapaxes(grad_part, 0, 1).astype(jnp.float32) * attended, -1)
    grad_score = (probability * (grad_prob - row_delta[..., None])).astype(jnp.bfloat16)
    grad_query = (
        jnp.einsum("hrk,khc->rhc", grad_score, key_part, preferred_element_type=jnp.float32)
        * score_scale
    ).astype(jnp.bfloat16)
    grad_key = (
        jnp.einsum("hrk,rhc->khc", grad_score, query_part, preferred_element_type=jnp.float32)
        * score_scale
    ).astype(jnp.bfloat16)
    grad_value = jnp.einsum(
        "hrk,rhc->khc", rounded_prob, grad_part, preferred_element_type=jnp.float32
    ).astype(jnp.bfloat16)
    key_mass = jnp.sum(probability, (0, 1))
    return (grad_query, grad_key, grad_value, key_mass)


def attend_local(queries_here, grads_here, received, owners):
    question_count, answer_rows, width_here = queries_here.shape
    slot_count, _, tile_rows, _ = received.shape
    row_count = question_count * answer_rows
    key_count = slot_count * tile_rows
    local_heads = width_here // HD
    group_heads = math.gcd(8, local_heads)
    group_count = local_heads // group_heads
    score_scale = 1.0 / math.sqrt(HD)
    row_owner = jnp.arange(row_count, dtype=jnp.int32) // answer_rows
    key_owner = jnp.repeat(owners, tile_rows)
    allowed = row_owner[:, None] == key_owner[None, :]

    def split_heads(values, count):
        return jnp.moveaxis(values.reshape(count, group_count, group_heads, HD), 1, 0)

    query_groups = split_heads(queries_here.reshape(row_count, width_here), row_count)
    grad_groups = split_heads(grads_here.reshape(row_count, width_here), row_count)
    key_groups = split_heads(received[:, 0].reshape(key_count, width_here), key_count)
    value_groups = split_heads(received[:, 1].reshape(key_count, width_here), key_count)

    def one_group(pieces):
        return head_block(pieces, allowed, score_scale)

    grad_query, grad_key, grad_value, key_mass = lax.map(
        one_group, (query_groups, key_groups, value_groups, grad_groups)
    )
    grad_query = jnp.moveaxis(grad_query, 0, 1).reshape(question_count, answer_rows, width_here)
    grad_key = jnp.moveaxis(grad_key, 0, 1).reshape(slot_count, tile_rows, width_here)
    grad_value = jnp.moveaxis(grad_value, 0, 1).reshape(slot_count, tile_rows, width_here)
    slot_mass = jnp.sum(key_mass, 0).reshape(slot_count, tile_rows).sum(-1)
    return (grad_query, jnp.stack([grad_key, grad_value], 1), slot_mass)


def slot_owners(passage_slot, passage_question, source, decoder, n_devices, per_device, per_pair):
    source_start = source * n_devices * per_device
    table_slot = lax.dynamic_slice_in_dim(
        passage_slot, source_start, n_devices * per_device
    ).reshape(n_devices, per_device)
    table_question = lax.dynamic_slice_in_dim(
        passage_question, source_start, n_devices * per_device
    ).reshape(n_devices, per_device)
    wanted = decoder * per_pair + jnp.arange(per_pair, dtype=jnp.int32)
    matches = table_slot[:, None, :] == wanted[None, :, None]
    owner_ids = jnp.sum(jnp.where(matches, table_question[:, None, :], 0), -1)
    return jnp.where(jnp.any(matches, -1), owner_ids, -1).reshape(n_devices * per_pair)


def body(queries, keys_values, cotangent, passage_slot, passage_question):
    n_devices = lax.axis_size("dp")
    section = lax.axis_index("sec")
    decoder = lax.axis_index("dp")
    per_device = keys_values.shape[0]
    per_pair = SLOTS // n_devices
    my_start = (section * n_devices + decoder) * per_device
    my_slots = lax.dynamic_slice_in_dim(passage_slot, my_start, per_device)
    placing = (jnp.arange(SLOTS, dtype=jnp.int32)[:, None] == my_slots[None, :]).astype(
        jnp.bfloat16
    )
    other_section = 1 - section
    outgoing = jnp.einsum(
        "sj,jkld->skld", placing, keys_values, preferred_element_type=jnp.float32
    ).astype(jnp.bfloat16)
    received = lax.all_to_all(outgoing, "dp", split_axis=0, concat_axis=0, tiled=True)
    received = partner(received, "sec", 0)
    queries_here, grads_here = (queries, cotangent)
    owners = slot_owners(
        passage_slot, passage_question, other_section, decoder, n_devices, per_device, per_pair
    )
    grad_queries, grad_slots, slot_mass = attend_local(queries_here, grads_here, received, owners)
    total_mass = lax.psum(slot_mass, "mp")
    slot_relevance = (total_mass / (HEADS * ANS)).astype(jnp.bfloat16)
    grad_slots, slot_relevance = partner((grad_slots, slot_relevance), "sec", 0)
    returned, relevance_back = (
        lax.all_to_all(grad_slots, "dp", split_axis=0, concat_axis=0, tiled=True),
        lax.all_to_all(slot_relevance, "dp", split_axis=0, concat_axis=0, tiled=True),
    )
    grad_tiles = jnp.einsum(
        "sj,skld->jkld", placing, returned, preferred_element_type=jnp.float32
    ).astype(jnp.bfloat16)
    relevance = jnp.einsum(
        "sj,s->j", placing, relevance_back, preferred_element_type=jnp.float32
    ).astype(jnp.bfloat16)
    return (grad_queries, grad_tiles, relevance)


def solution(mesh):
    return jax.shard_map(
        body,
        mesh=mesh,
        in_specs=(
            P(("sec", "dp"), None, "mp"),
            P(("sec", "dp"), None, None, "mp"),
            P(("sec", "dp"), None, "mp"),
            P(),
            P(),
        ),
        out_specs=(
            P(("sec", "dp"), None, "mp"),
            P(("sec", "dp"), None, None, "mp"),
            P(("sec", "dp")),
        ),
        check_vma=False,
    )
```

profile of v0, /device:TPU:29, one launch (start us, length us, event | category | flops | bytes accessed | tf_op | source)
XLA Modules:
  0.0 1190.7 jit_solution(9637078979443288547)
XLA Ops:
  2.0 10.5 convolution_convert_fusion
  12.5 11.2 copy.40
  23.7 200.9 %all_to_all.23 = bf16[32,2,32,2048]{3,2,1,0:T(8,128)(2,1)} all-to-all(bf16[32,2,32,2048]{3,2,1,0:T(8,128)(2,1)} %copy.40), channel_id=1, replica_groups=mesh['sec'=2,'dp'=8,'mp'=2] {'dp'}, dimensions={0} | all-to-all | bytes 16777216 | tf_op jit(solution)/shard_map/all_to_all | solution.py:115
  240.7 165.8 %collective-permute-done = bf16[32,2,32,2048]{3,2,1,0:T(8,128)(2,1)} collective-permute-done((bf16[32,2,32,2048]{3,2,1,0:T(8,128)(2,1)}, bf16[32,2,32,2048]{3,2,1,0:T(8,128)(2,1)}, u32[]{:S(2)}, u32[]{:S(2)}) %collective-permute-start) | collective-permute-done | bytes 8388640 | tf_op jit(solution)/shard_map/ppermute | solution.py:15
  412.5 12.9 %reshape_reshape_squeeze.6 = bf16[1024,4,8,64]{3,2,1,0:T(8,128)(2,1)} reshape(bf16[32,1,32,2048]{3,2,1,0:T(8,128)(2,1)} %get-tuple-element.158) | data formatting | bytes 8388608 | tf_op jit(solution)/shard_map/reshape;reshape;squeeze | solution.py:66
  425.4 9.8 copy.44
  435.2 12.9 %reshape_reshape_squeeze.7 = bf16[1024,4,8,64]{3,2,1,0:T(8,128)(2,1)} reshape(bf16[32,1,32,2048]{3,2,1,0:T(8,128)(2,1)} %get-tuple-element.157) | data formatting | bytes 8388608 | tf_op jit(solution)/shard_map/reshape;reshape;squeeze | solution.py:66
  448.1 9.8 copy.45
  457.9 274.7 %while.17 = (s32[]{:T(128)}, bf16[4,512,8,64]{1,3,2,0:T(8,128)(2,1)}, bf16[4,1024,8,64]{1,3,2,0:T(8,128)(2,1)}, bf16[4,1024,8,64]{1,3,2,0:T(8,128)(2,1)}, f32[4,...) while((s32[]{:T(128)}, ...), condition=%wide.region_7.8_spmd.clone, body=%wide.region_2.7_spmd.clone.sunk | while | flops 3291738112 | bytes 228729008 | solution.py:76
  457.9 9.3 fusion.110
  467.6 21.1 %fusion.111 = (f32[8,512]{1,0:T(8,128)S(1)}, f32[8,512,1024]{2,1,0:T(8,128)}) fusion(f32[8,512,1024]{2,1,0:T(8,128)} %fusion.110, pred[512,1024]{1,0:T(8,128)(4,1)S(1)} %broadcast_compare_fusion.2), kind=kOutput, calls=%fused_computation.79.clone.1 | output fusion | flops 25166848 | bytes 34095104 | tf_op jit(solution)/shard_map/while/body/eval_jaxpr/sub | solution.py:26
  495.5 8.7 fusion.115
  511.5 7.7 multiply_convert_fusion.4
  526.5 9.3 fusion.110
  536.1 21.1 %fusion.111 = (f32[8,512]{1,0:T(8,128)S(1)}, f32[8,512,1024]{2,1,0:T(8,128)}) fusion(f32[8,512,1024]{2,1,0:T(8,128)} %fusion.110, pred[512,1024]{1,0:T(8,128)(4,1)S(1)} %broadcast_compare_fusion.2), kind=kOutput, calls=%fused_computation.79.clone.1 | output fusion | flops 25166848 | bytes 34095104 | tf_op jit(solution)/shard_map/while/body/eval_jaxpr/sub | solution.py:26
  564.1 8.7 fusion.115
  580.1 7.7 multiply_convert_fusion.4
  595.0 9.3 fusion.110
  604.7 21.1 %fusion.111 = (f32[8,512]{1,0:T(8,128)S(1)}, f32[8,512,1024]{2,1,0:T(8,128)}) fusion(f32[8,512,1024]{2,1,0:T(8,128)} %fusion.110, pred[512,1024]{1,0:T(8,128)(4,1)S(1)} %broadcast_compare_fusion.2), kind=kOutput, calls=%fused_computation.79.clone.1 | output fusion | flops 25166848 | bytes 34095104 | tf_op jit(solution)/shard_map/while/body/eval_jaxpr/sub | solution.py:26
  632.7 8.7 fusion.115
  663.6 9.3 fusion.110
  673.3 21.1 %fusion.111 = (f32[8,512]{1,0:T(8,128)S(1)}, f32[8,512,1024]{2,1,0:T(8,128)}) fusion(f32[8,512,1024]{2,1,0:T(8,128)} %fusion.110, pred[512,1024]{1,0:T(8,128)(4,1)S(1)} %broadcast_compare_fusion.2), kind=kOutput, calls=%fused_computation.79.clone.1 | output fusion | flops 25166848 | bytes 34095104 | tf_op jit(solution)/shard_map/while/body/eval_jaxpr/sub | solution.py:26
  701.2 8.7 fusion.115
  717.2 7.7 multiply_convert_fusion.4
  732.6 12.9 %copy.46 = bf16[1024,4,8,64]{3,2,1,0:T(8,128)(2,1)} copy(bf16[1024,4,8,64]{0,3,2,1:T(8,128)(2,1)} %bitcast.8) | data formatting | bytes 8388608 | tf_op jit(solution)/shard_map/transpose | solution.py:80
  745.5 12.3 %stack_reshape.6 = bf16[32,1,32,2048]{3,2,0,1:T(8,128)(2,1)} reshape(bf16[1024,4,8,64]{3,2,1,0:T(8,128)(2,1)} %copy.46) | data formatting | bytes 8388608 | tf_op jit(solution)/shard_map/stack;reshape | solution.py:83
  757.8 12.9 %copy.47 = bf16[1024,4,8,64]{3,2,1,0:T(8,128)(2,1)} copy(bf16[1024,4,8,64]{0,3,2,1:T(8,128)(2,1)} %bitcast.113) | data formatting | bytes 8388608 | tf_op jit(solution)/shard_map/transpose | solution.py:81
  770.7 12.3 %stack_reshape.7 = bf16[32,1,32,2048]{3,2,0,1:T(8,128)(2,1)} reshape(bf16[1024,4,8,64]{3,2,1,0:T(8,128)(2,1)} %copy.47) | data formatting | bytes 8388608 | tf_op jit(solution)/shard_map/stack;reshape | solution.py:83
  796.1 175.4 %collective-permute-done.2 = bf16[32]{0:T(256)(128)(2,1)S(1)} collective-permute-done((bf16[32]{0:T(256)(128)(2,1)S(1)}, bf16[32]{0:T(256)(128)(2,1)S(1)}, u32[]{:S(2)}, u32[]{:S(2)}) %collective-permute-start.2) | collective-permute-done | bytes 96 | tf_op jit(solution)/shard_map/ppermute | solution.py:15
  979.1 8.3 copy.48
  998.6 175.3 %all-to-all-done.1 = bf16[32,2,32,2048]{3,2,1,0:T(8,128)(2,1)} async-done(((bf16[32,2,32,2048]{3,2,1,0:T(8,128)(2,1)}), bf16[32,2,32,2048]{3,2,1,0:T(8,128)(2,1)}, u32[]{:S(2)}, u32[]{:S(2)}) %all-to-all-start.1) | async-done | bytes 8388640 | tf_op jit(solution)/shard_map/all_to_all | solution.py:126
  1173.9 12.4 %fusion.60 = bf16[16,2,32,2048]{3,0,2,1:T(8,128)(2,1)S(1)} fusion(bf16[32,2,32,2048]{3,2,1,0:T(8,128)(2,1)} %all-to-all-done.1, s32[16]{0:T(128)S(1)} %copy-done.4), kind=kOutput, calls=%fused_computation.58 | convolution fusion | flops 136315392 | bytes 12582976 | tf_op jit(solution)/shard_map/sj,skld->jkld/dot_general | solution.py:129
  (94 shorter events, 154.3 us)
Async XLA Ops:
  1.4 0.6 copy-start.3
  23.7 202.1 %copy-start.5 = (s32[256]{0:T(256)S(1)}, s32[256]{0:T(256)}, u32[]{:S(2)}) copy-start(s32[256]{0:T(256)} %param.10) | copy-start | bytes 3076
  23.7 202.3 %copy-start.6 = (s32[256]{0:T(256)S(1)}, s32[256]{0:T(256)}, u32[]{:S(2)}) copy-start(s32[256]{0:T(256)} %param.11) | copy-start | bytes 3076
  23.7 203.2 %copy-start.1 = (bf16[4,128,2048]{2,1,0:T(8,128)(2,1)S(1)}, bf16[4,128,2048]{2,1,0:T(8,128)(2,1)}, u32[]{:S(2)}) copy-start(bf16[4,128,2048]{2,1,0:T(8,128)(2,1)} %param.7) | copy-start | bytes 6291460
  224.6 181.9 %collective-permute-start = (bf16[32,2,32,2048]{3,2,1,0:T(8,128)(2,1)}, bf16[32,2,32,2048]{3,2,1,0:T(8,128)(2,1)}, u32[]{:S(2)}, u32[]{:S(2)}) collective-permute-start(bf16[32,2,32,2048]{3,2,1,0:T(8,128)(2,1)} %all_to_all.23), channel_id=1, source_target_pairs={{0,16},{16,0},{1,17},{17,1},{2,18},{18,2},{3,19},{19,3},{4,20},{20... | collective-permute-start | bytes 25165832 | tf_op jit(solution)/shard_map/ppermute | solution.py:15
  495.5 11.1 copy-start
  495.5 11.7 copy-start.2
  564.1 11.1 copy-start
  564.1 11.7 copy-start.2
  632.7 11.1 copy-start
  632.7 11.7 copy-start.2
  701.2 11.1 copy-start
  701.2 11.7 copy-start.2
  790.5 188.6 %collective-permute-start.1 = (bf16[32,2,32,2048]{3,2,0,1:T(8,128)(2,1)}, bf16[32,2,32,2048]{3,2,0,1:T(8,128)(2,1)}, u32[]{:S(2)}, u32[]{:S(2)}) collective-permute-start(bf16[32,2,32,2048]{3,2,0,1:T(8,128)(2,1)} %pad_maximum_fusion), channel_id=1, source_target_pairs={{0,16},{16,0},{1,17},{17,1},{2,18},{18,2},{3,19},{19,3},{4,20},{20... | collective-permute-start | bytes 25165832 | tf_op jit(solution)/shard_map/ppermute | solution.py:15
  796.1 175.4 %collective-permute-start.2 = (bf16[32]{0:T(256)(128)(2,1)S(1)}, bf16[32]{0:T(256)(128)(2,1)S(1)}, u32[]{:S(2)}, u32[]{:S(2)}) collective-permute-start(bf16[32]{0:T(256)(128)(2,1)S(1)} %multiply_convert_fusion.2), channel_id=1, source_target_pairs={{0,16},{16,0},{1,17},{17,1},{2,18},{18,2},{3,19},{19,3},{4,20},{20... | collective-permute-start | bytes 200 | tf_op jit(solution)/shard_map/ppermute | solution.py:15
  972.2 15.2 %all-to-all-start.2 = ((bf16[8,4,1]{1,2,0:T(2,128)(2,1)}), bf16[8,4,1]{1,2,0:T(2,128)(2,1)S(1)}, u32[]{:S(2)}, u32[]{:S(2)}) async-start(bf16[8,4,1]{1,2,0:T(2,128)(2,1)} %all_to_all.19), calls=%async_computation.2 | async-start | bytes 8192 | tf_op jit(solution)/shard_map/all_to_all | solution.py:127
  987.4 186.4 %all-to-all-start.1 = ((bf16[32,2,32,2048]{3,2,1,0:T(8,128)(2,1)}), bf16[32,2,32,2048]{3,2,1,0:T(8,128)(2,1)}, u32[]{:S(2)}, u32[]{:S(2)}) async-start(bf16[32,2,32,2048]{3,2,1,0:T(8,128)(2,1)} %copy.48), calls=%async_computation.1 | async-start | bytes 16777216 | tf_op jit(solution)/shard_map/all_to_all | solution.py:126
  992.5 5.4 copy-start.4
where the time goes:
time: 1200 us; the launch traced here: 1190 us
  waiting for transfers between devices  516 us (43%)
  blocking collectives  205 us (17%)
  matrix products  173 us (14%)
  local copies, waits for them, and re-layouts  160 us (13%)
  other arithmetic  121 us (10%)
  starting transfers between devices  14.5 us (1%)
    ppermute x3, waiting for transfers between devices, partner(): lax.ppermute(x, axis, [(i, i ^ 1 << distance) for i in range(lax.axis_siz...  341 us
    all_to_all x1, blocking collectives, body(): lax.all_to_all(outgoing, 'dp', split_axis=0, concat_axis=0, tiled=True)  201 us
    all_to_all x1, waiting for transfers between devices, body(): lax.all_to_all(grad_slots, 'dp', split_axis=0, concat_axis=0, tiled=True)  175 us
    sub x4, other arithmetic, head_block(): exponent = jnp.exp(scores - row_max)  84.3 us
    dot_general x4, matrix products, head_block(): jnp.einsum('rhc,khc->hrk', query_part, key_part, preferred_element_type=j...  37.2 us
    dot_general x4, matrix products, head_block(): jnp.einsum('hrk,rhc->khc', rounded_prob, grad_part, preferred_element_typ...  34.9 us
    unnamed x16, local copies, waits for them, and re-layouts  34.1 us
    another operation x4, local copies, waits for them, and re-layouts, split_heads(): values.reshape(count, group_count, group_heads, HD)  32.6 us
  transfers between devices with their start and end apart: 5, of which 3 were waited for; matrix products, arithmetic and copies ran while one was open for 2% of the time, Pallas kernels for 0%

commit v1 on v0

v1 whole, which is shorter than its diff:
```python
import functools
import math

import jax
import jax.numpy as jnp
from jax import lax
from jax.experimental import pallas as pl
from jax.experimental.pallas import tpu as pltpu
from jax.sharding import PartitionSpec as P

HEADS = 64
HD = 64
ANS = 128
SLOTS = 32
LANES = 128
CHUNKS = 4
GROUP = 8
MESH = pl.DeviceIdType.MESH
VMEM_LIMIT = 48 * 1024 * 1024


def remote(src, dst, send_sem, recv_sem, where):
    return pltpu.make_async_remote_copy(
        src_ref=src,
        dst_ref=dst,
        send_sem=send_sem,
        recv_sem=recv_sem,
        device_id=where,
        device_id_type=MESH,
    )


def greet(targets):
    barrier = pltpu.get_barrier_semaphore()
    for where in targets:
        pl.semaphore_signal(barrier, inc=1, device_id=where, device_id_type=MESH)
    pl.semaphore_wait(barrier, len(targets))


def dispatch_kernel(
    n, index_ref, kv_ref, recv_ref, mid, out, x_send, x_recv, z_send, z_recv, own_sem
):
    section = lax.axis_index("sec")
    me = lax.axis_index("dp")
    per_pair = SLOTS // n
    columns = kv_ref.shape[3] // CHUNKS
    peers = [lax.rem(me + d, n) for d in range(1, n)]
    across = {"sec": 1 - section}
    greet([across] + [{"dp": peer} for peer in peers])

    crossing = []
    for c in range(CHUNKS):
        copy = remote(
            kv_ref.at[:, :, :, pl.ds(c * columns, columns)],
            mid[c],
            x_send.at[c],
            x_recv.at[c],
            across,
        )
        copy.start()
        crossing.append(copy)
    sends = []
    locals_ = []
    my_rows = pl.ds(me * per_pair, per_pair)
    for c in range(CHUNKS):
        crossing[c].wait_recv()

        def place(s, carry):
            out[c, s] = mid[c][index_ref[s]]
            return carry

        lax.fori_loop(0, SLOTS, place, 0)
        for d, peer in enumerate(peers, 1):
            copy = remote(
                out.at[c, pl.ds(peer * per_pair, per_pair)],
                recv_ref.at[c, my_rows],
                z_send.at[c, d],
                z_recv.at[c, d],
                {"dp": peer},
            )
            copy.start()
            sends.append(copy)
        copy = pltpu.make_async_copy(out.at[c, my_rows], recv_ref.at[c, my_rows], own_sem.at[c])
        copy.start()
        locals_.append(copy)
    for c in range(CHUNKS):
        crossing[c].wait_send()
        locals_[c].wait()
        for d in range(1, n):
            source = lax.rem(me + n - d, n)
            landed = recv_ref.at[c, pl.ds(source * per_pair, per_pair)]
            remote(landed, landed, z_send.at[c, d], z_recv.at[c, d], {"dp": source}).wait_recv()
    for copy in sends:
        copy.wait_send()


def dispatch(keys_values, index):
    n = lax.axis_size("dp")
    count, _, rows, width = keys_values.shape
    columns = width // CHUNKS
    return pl.pallas_call(
        functools.partial(dispatch_kernel, n),
        out_shape=jax.ShapeDtypeStruct((CHUNKS, SLOTS, 2, rows, columns), jnp.bfloat16),
        in_specs=[
            pl.BlockSpec(memory_space=pltpu.SMEM),
            pl.BlockSpec(memory_space=pl.ANY),
        ],
        out_specs=pl.BlockSpec(memory_space=pl.ANY),
        scratch_shapes=[
            [pltpu.VMEM((count, 2, rows, columns), jnp.bfloat16)] * CHUNKS,
            pltpu.VMEM((CHUNKS, SLOTS, 2, rows, columns), jnp.bfloat16),
            pltpu.SemaphoreType.DMA((CHUNKS,)),
            pltpu.SemaphoreType.DMA((CHUNKS,)),
            pltpu.SemaphoreType.DMA((CHUNKS, n)),
            pltpu.SemaphoreType.DMA((CHUNKS, n)),
            pltpu.SemaphoreType.DMA((CHUNKS,)),
        ],
        compiler_params=pltpu.CompilerParams(
            collective_id=0, has_side_effects=True, vmem_limit_bytes=VMEM_LIMIT
        ),
    )(index, keys_values)


def collect_kernel(
    n,
    slot_ref,
    grads_ref,
    mass_ref,
    tiles_ref,
    total_ref,
    back,
    dense,
    mass_back,
    mass_dense,
    mass_here,
    mass_other,
    z_send,
    z_recv,
    own_sem,
    x_send,
    x_recv,
    m_send,
    m_recv,
    small_send,
    small_recv,
):
    section = lax.axis_index("sec")
    me = lax.axis_index("dp")
    half = lax.axis_index("mp")
    per_pair = SLOTS // n
    count = dense.shape[1]
    columns = dense.shape[4]
    peers = [lax.rem(me + d, n) for d in range(1, n)]
    across = {"sec": 1 - section}
    beside = {"mp": 1 - half}
    greet([across, beside] + [{"dp": peer} for peer in peers])

    my_rows = pl.ds(me * per_pair, per_pair)
    sends = []
    locals_ = []
    for d, peer in enumerate(peers, 1):
        copy = remote(
            mass_ref.at[pl.ds(peer * per_pair, per_pair)],
            mass_back.at[my_rows],
            m_send.at[d],
            m_recv.at[d],
            {"dp": peer},
        )
        copy.start()
        sends.append(copy)
    own_mass = pltpu.make_async_copy(mass_ref.at[my_rows], mass_back.at[my_rows], own_sem.at[CHUNKS])
    own_mass.start()
    for c in range(CHUNKS):
        for d, peer in enumerate(peers, 1):
            copy = remote(
                grads_ref.at[c, pl.ds(peer * per_pair, per_pair)],
                back[c].at[my_rows],
                z_send.at[c, d],
                z_recv.at[c, d],
                {"dp": peer},
            )
            copy.start()
            sends.append(copy)
        copy = pltpu.make_async_copy(grads_ref.at[c, my_rows], back[c].at[my_rows], own_sem.at[c])
        copy.start()
        locals_.append(copy)

    def arrived(buffer, send_sem, recv_sem, d):
        source = lax.rem(me + n - d, n)
        landed = buffer.at[pl.ds(source * per_pair, per_pair)]
        remote(landed, landed, send_sem, recv_sem, {"dp": source}).wait_recv()

    own_mass.wait()
    for d in range(1, n):
        arrived(mass_back, m_send.at[d], m_recv.at[d], d)

    def pick_mass(j, carry):
        mass_dense[j] = mass_back[slot_ref[j]]
        return carry

    lax.fori_loop(0, count, pick_mass, 0)
    first = remote(mass_dense, mass_here, small_send.at[0], small_recv.at[0], across)
    first.start()

    crossing = []
    second = None
    for c in range(CHUNKS):
        locals_[c].wait()
        for d in range(1, n):
            arrived(back[c], z_send.at[c, d], z_recv.at[c, d], d)

        def pick(j, carry):
            dense[c, j] = back[c][slot_ref[j]]
            return carry

        lax.fori_loop(0, count, pick, 0)
        copy = remote(
            dense.at[c],
            tiles_ref.at[:, :, :, pl.ds(c * columns, columns)],
            x_send.at[c],
            x_recv.at[c],
            across,
        )
        copy.start()
        crossing.append(copy)
        if c == 0:
            first.wait_recv()
            second = remote(mass_here, mass_other, small_send.at[1], small_recv.at[1], beside)
            second.start()
    second.wait()
    total_ref[...] = mass_here[...] + mass_other[...]
    first.wait_send()
    for copy in crossing:
        copy.wait()
    for copy in sends:
        copy.wait_send()


def collect(slots, grads, mass, count):
    n = lax.axis_size("dp")
    _, _, _, rows, columns = grads.shape
    small = pltpu.VMEM((count, 8, LANES), jnp.float32)
    return pl.pallas_call(
        functools.partial(collect_kernel, n),
        out_shape=(
            jax.ShapeDtypeStruct((count, 2, rows, columns * CHUNKS), jnp.bfloat16),
            jax.ShapeDtypeStruct((count, 8, LANES), jnp.float32),
        ),
        in_specs=[
            pl.BlockSpec(memory_space=pltpu.SMEM),
            pl.BlockSpec(memory_space=pl.ANY),
            pl.BlockSpec(memory_space=pl.ANY),
        ],
        out_specs=(
            pl.BlockSpec(memory_space=pl.ANY),
            pl.BlockSpec(memory_space=pltpu.VMEM),
        ),
        scratch_shapes=[
            [pltpu.VMEM((SLOTS, 2, rows, columns), jnp.bfloat16)] * CHUNKS,
            pltpu.VMEM((CHUNKS, count, 2, rows, columns), jnp.bfloat16),
            pltpu.VMEM((SLOTS, 8, LANES), jnp.float32),
            small,
            small,
            small,
            pltpu.SemaphoreType.DMA((CHUNKS, n)),
            pltpu.SemaphoreType.DMA((CHUNKS, n)),
            pltpu.SemaphoreType.DMA((CHUNKS + 1,)),
            pltpu.SemaphoreType.DMA((CHUNKS,)),
            pltpu.SemaphoreType.DMA((CHUNKS,)),
            pltpu.SemaphoreType.DMA((n,)),
            pltpu.SemaphoreType.DMA((n,)),
            pltpu.SemaphoreType.DMA((2,)),
            pltpu.SemaphoreType.DMA((2,)),
        ],
        compiler_params=pltpu.CompilerParams(
            collective_id=1, has_side_effects=True, vmem_limit_bytes=VMEM_LIMIT
        ),
    )(slots, grads, mass)


def stack_heads(pair):
    lane = lax.broadcasted_iota(jnp.int32, pair.shape, 1)
    zero = jnp.zeros_like(pair)
    return jnp.concatenate([jnp.where(lane < HD, pair, zero), jnp.where(lane < HD, zero, pair)], 0)


def attend_kernel(
    rank_ref,
    start_ref,
    count_ref,
    query_ref,
    cot_ref,
    recv_ref,
    grad_query_ref,
    grad_ref,
    mass_out_ref,
    keys,
    values,
    grad_keys,
    grad_values,
    mass,
):
    step = pl.program_id(0)
    questions, _, columns = query_ref.shape
    rows = recv_ref.shape[3]
    pairs = columns // LANES
    scale = 1.0 / math.sqrt(HD)

    @pl.when(step == 0)
    def _():
        mass[...] = jnp.zeros_like(mass)

    tail = pl.ds(SLOTS * rows, GROUP * rows)
    keys[tail, :] = jnp.zeros((GROUP * rows, columns), keys.dtype)
    values[tail, :] = jnp.zeros((GROUP * rows, columns), values.dtype)

    def sort_in(s, carry):
        at = pl.ds(pl.multiple_of(rank_ref[s] * rows, rows), rows)
        keys[at, :] = recv_ref[0, s, 0]
        values[at, :] = recv_ref[0, s, 1]
        return carry

    lax.fori_loop(0, SLOTS, sort_in, 0)

    def one(t, carry):
        question = t // pairs
        lanes = pl.ds(pl.multiple_of((t % pairs) * LANES, LANES), LANES)
        start = start_ref[question]
        held = count_ref[question]
        blocks = (held + GROUP - 1) // GROUP

        def run(block_count):
            size = block_count * GROUP * rows
            window = pl.ds(pl.multiple_of(start * rows, rows), size)
            query = stack_heads(query_ref[question, :, lanes] * jnp.asarray(scale, jnp.bfloat16))
            cot = stack_heads(cot_ref[question, :, lanes])
            key = keys[window, lanes]
            value = values[window, lanes]
            last = (((1,), (1,)), ((), ()))
            score = lax.dot_general(key, query, last, preferred_element_type=jnp.float32)
            row = lax.broadcasted_iota(jnp.int32, score.shape, 0)
            score = jnp.where(row < held * rows, score, -jnp.inf)
            exponent = jnp.exp(score - jnp.max(score, 0, keepdims=True))
            prob = exponent * (1.0 / jnp.sum(exponent, 0, keepdims=True))
            rounded = prob.astype(jnp.bfloat16)
            folded = prob.reshape(block_count * GROUP, rows // 8, 8, prob.shape[1]).sum(1)
            mass[pl.ds(start, block_count * GROUP)] += folded
            grad_prob = lax.dot_general(value, cot, last, preferred_element_type=jnp.float32)
            delta = jnp.sum(rounded.astype(jnp.float32) * grad_prob, 0, keepdims=True)
            grad_score = (prob * (grad_prob - delta)).astype(jnp.bfloat16)
            grad_keys[window, lanes] = jnp.dot(
                grad_score, query, preferred_element_type=jnp.float32
            ).astype(jnp.bfloat16)
            grad_values[window, lanes] = jnp.dot(
                rounded, cot, preferred_element_type=jnp.float32
            ).astype(jnp.bfloat16)
            turned = lax.dot_general(
                key, grad_score, (((0,), (0,)), ((), ())), preferred_element_type=jnp.float32
            )
            answer = turned.shape[1] // 2
            both = jnp.concatenate([turned[:HD, :answer], turned[HD:, answer:]], 0)
            grad_query_ref[question, :, lanes] = (both.T * scale).astype(jnp.bfloat16)

        for block_count in range(1, SLOTS // GROUP + 1):
            pl.when(blocks == block_count)(functools.partial(run, block_count))
        return carry

    lax.fori_loop(0, questions * pairs, one, 0)

    def sort_out(s, carry):
        at = pl.ds(pl.multiple_of(rank_ref[s] * rows, rows), rows)
        grad_ref[0, s, 0] = grad_keys[at, :]
        grad_ref[0, s, 1] = grad_values[at, :]
        return carry

    lax.fori_loop(0, SLOTS, sort_out, 0)

    @pl.when(step == pl.num_programs(0) - 1)
    def _():
        def fold(s, carry):
            part = mass[rank_ref[s]]
            mass_out_ref[s] = part[:, :LANES] + part[:, LANES:]
            return carry

        lax.fori_loop(0, SLOTS, fold, 0)


def attend(queries, cotangent, received, rank, starts, counts):
    questions, answer, width = queries.shape
    _, _, _, rows, columns = received.shape
    total = (SLOTS + GROUP) * rows
    side = pl.BlockSpec((questions, answer, columns), lambda c, *_: (0, 0, c))
    tiles = pl.BlockSpec((1, SLOTS, 2, rows, columns), lambda c, *_: (c, 0, 0, 0, 0))
    held = pltpu.VMEM((total, columns), jnp.bfloat16)
    return pl.pallas_call(
        attend_kernel,
        grid_spec=pltpu.PrefetchScalarGridSpec(
            num_scalar_prefetch=3,
            grid=(CHUNKS,),
            in_specs=[side, side, tiles],
            out_specs=(
                side,
                tiles,
                pl.BlockSpec((SLOTS, 8, LANES), lambda c, *_: (0, 0, 0)),
            ),
            scratch_shapes=[
                held,
                held,
                held,
                held,
                pltpu.VMEM((SLOTS + GROUP, 8, 2 * answer), jnp.float32),
            ],
        ),
        out_shape=(
            jax.ShapeDtypeStruct(queries.shape, jnp.bfloat16),
            jax.ShapeDtypeStruct(received.shape, jnp.bfloat16),
            jax.ShapeDtypeStruct((SLOTS, 8, LANES), jnp.float32),
        ),
        compiler_params=pltpu.CompilerParams(vmem_limit_bytes=VMEM_LIMIT),
    )(rank, starts, counts, queries, cotangent, received)


def slot_owners(passage_slot, passage_question, source, decoder, n_devices, per_device, per_pair):
    source_start = source * n_devices * per_device
    table_slot = lax.dynamic_slice_in_dim(
        passage_slot, source_start, n_devices * per_device
    ).reshape(n_devices, per_device)
    table_question = lax.dynamic_slice_in_dim(
        passage_question, source_start, n_devices * per_device
    ).reshape(n_devices, per_device)
    wanted = decoder * per_pair + jnp.arange(per_pair, dtype=jnp.int32)
    matches = table_slot[:, None, :] == wanted[None, :, None]
    owner_ids = jnp.sum(jnp.where(matches, table_question[:, None, :], 0), -1)
    return jnp.where(jnp.any(matches, -1), owner_ids, -1).reshape(n_devices * per_pair)


def body(queries, keys_values, cotangent, passage_slot, passage_question):
    n_devices = lax.axis_size("dp")
    section = lax.axis_index("sec")
    index = lax.axis_index("dp")
    per_device = keys_values.shape[0]
    questions = queries.shape[0]
    per_pair = SLOTS // n_devices
    other_section = 1 - section
    start = (other_section * n_devices + index) * per_device
    slots = lax.dynamic_slice_in_dim(passage_slot, start, per_device)
    numbers = jnp.arange(SLOTS, dtype=jnp.int32)
    places = jnp.arange(per_device, dtype=jnp.int32)
    passage_of = jnp.sum(jnp.where(slots[None, :] == numbers[:, None], places[None, :], 0), -1)
    owners = slot_owners(
        passage_slot, passage_question, other_section, index, n_devices, per_device, per_pair
    )
    order_key = jnp.where(owners < 0, questions, owners) * SLOTS + numbers
    rank = jnp.sum((order_key[None, :] < order_key[:, None]).astype(jnp.int32), -1)
    asked = jnp.arange(questions, dtype=jnp.int32)
    counts = jnp.sum((owners[None, :] == asked[:, None]).astype(jnp.int32), -1)
    starts = jnp.sum((order_key[None, :] < asked[:, None] * SLOTS).astype(jnp.int32), -1)

    received = dispatch(keys_values, passage_of)
    grad_queries, grads, mass = attend(queries, cotangent, received, rank, starts, counts)
    grad_tiles, total = collect(slots, grads, mass, per_device)
    relevance = (jnp.sum(total, (1, 2)) / (HEADS * ANS)).astype(jnp.bfloat16)
    return (grad_queries, grad_tiles, relevance)


def solution(mesh):
    return jax.shard_map(
        body,
        mesh=mesh,
        in_specs=(
            P(("sec", "dp"), None, "mp"),
            P(("sec", "dp"), None, None, "mp"),
            P(("sec", "dp"), None, "mp"),
            P(),
            P(),
        ),
        out_specs=(
            P(("sec", "dp"), None, "mp"),
            P(("sec", "dp"), None, None, "mp"),
            P(("sec", "dp")),
        ),
        check_vma=False,
    )
```

time: 1200 us -> 488 us (0.41)
  waiting for transfers between devices: 516 us -> 0 us
  Pallas kernels: 0 us -> 473 us
  blocking collectives: 205 us -> 0 us
  matrix products: 173 us -> 0 us
  local copies, waits for them, and re-layouts: 160 us -> 11.5 us
  other arithmetic: 121 us -> 1.63 us
  starting transfers between devices: 14.5 us -> 0 us
    pallas_call x0 -> x3, Pallas kernels: none -> 473 us  [the longest x1 210 us: dispatch(): pl.pallas_call(functools.partial(dispatch_kernel, n), out_shape=jax.Shape...]
    ppermute x3 -> x0, waiting for transfers between devices: 341 us -> none  [partner(): lax.ppermute(x, axis, [(i, i ^ 1 << distance) for i in range(lax.axis_siz...]
    all_to_all x1 -> x0, blocking collectives: 201 us -> none  [body(): lax.all_to_all(outgoing, 'dp', split_axis=0, concat_axis=0, tiled=True)]
    all_to_all x2 -> x0, waiting for transfers between devices: 175 us -> none  [the longest x1 175 us: body(): lax.all_to_all(grad_slots, 'dp', split_axis=0, concat_axis=0, tiled=True)]
    dot_general x27 -> x0, matrix products: 173 us -> none  [the longest x4 37.2 us: head_block(): jnp.einsum('rhc,khc->hrk', query_part, key_part, preferred_element_type=j...]
    sub x4 -> x0, other arithmetic: 84.3 us -> none  [head_block(): exponent = jnp.exp(scores - row_max)]
    another operation x6 -> x0, local copies, waits for them, and re-layouts: 57.3 us -> none  [the longest x4 32.6 us: split_heads(): values.reshape(count, group_count, group_heads, HD)]
    reduce_sum x6 -> x4, other arithmetic: 27.2 us -> 0.64 us  [the longest x1 0.2 us: body(): relevance = (jnp.sum(total, (1, 2)) / (HEADS * ANS)).astype(jnp.bfloat16)]
  transfers between devices with their start and end apart: 5 -> 0, of which waited for: 3 -> 0; matrix products, arithmetic and copies ran while one was open for 2% -> 0% of each run, Pallas kernels for 0% -> 0%
where the time goes in v1:
time: 488 us; the launch traced here: 487 us
  Pallas kernels  473 us (97%)
  local copies, waits for them, and re-layouts  11.5 us (2%)
    pallas_call x1, Pallas kernels, dispatch(): pl.pallas_call(functools.partial(dispatch_kernel, n), out_shape=jax.Shape...  210 us
    pallas_call x1, Pallas kernels, collect(): pl.pallas_call(functools.partial(collect_kernel, n), out_shape=(jax.Shape...  208 us
    pallas_call x1, Pallas kernels, attend(): pl.pallas_call(attend_kernel, grid_spec=pltpu.PrefetchScalarGridSpec(num_...  55.4 us

profile of v1, /device:TPU:29, one launch (start us, length us, event | category | flops | bytes accessed | tf_op | source)
XLA Modules:
  0.0 487.1 jit_solution(8225352135428879837)
XLA Ops:
  0.6 0.8 dynamic_slice.11.slot_ref
  1.4 0.8 dynamic_slice.10
  2.2 0.8 dynamic_slice.9
  2.9 0.1 select_reduce_fusion.index_ref
  3.0 0.1 eq.20
  3.1 0.2 compare_reduce_fusion
  3.3 0.1 broadcast_in_dim.43
  3.4 0.2 fusion
  3.6 0.1 copy.8
  3.7 0.1 select_n.49
  3.8 0.2 convert_reduce_fusion.1
  4.0 0.2 convert_reduce_fusion.rank_ref
  4.2 0.0 copy-start
  4.2 2.2 copy-done
  6.4 0.0 copy-start.2
  6.4 0.0 copy-start.3
  6.4 209.9 %shard_map.76.recv_ref = bf16[4,32,2,32,512]{4,3,2,1,0:T(8,128)(2,1)} custom-call(s32[32]{0:T(128)S(1)} %select_reduce_fusion.index_ref, bf16[16,2,32,2048]{3,2,1,0:T(8,128)(2,1)S(1)} %copy-done), custom_call_target="tpu_custom_call" | custom-call | tf_op jit(solution)/shard_map/pallas_call | solution.py:101
  216.3 0.0 copy-done.2
  216.3 0.0 copy-done.3
  216.3 55.4 %shard_map.77 = (bf16[4,128,2048]{2,1,0:T(8,128)(2,1)}, bf16[4,32,2,32,512]{4,3,2,1,0:T(8,128)(2,1)}, f32[32,8,128]{2,1,0:T(8,128)S(1)}) custom-call(s32[32]{0:T(128)S(1)} %convert_reduce_fusion.rank_ref, s32[4]{0:T(128)S(1)} %get-tuple-element.14.start_ref, s32[4]{0:T(128)S(1)} %get-tuple-element.13.count_ref, bf16[4,128,2048]{2,1,0:T(8,128)(2,1)S(1)} %copy-done.2, ...), custom_call_target="tpu_custom_call" | custom-call | tf_op jit(solution)/shard_map/pallas_call | solution.py:395
  271.8 207.9 %shard_map.78 = (bf16[16,2,32,2048]{3,2,1,0:T(8,128)(2,1)S(1)}, f32[16,8,128]{2,1,0:T(8,128)S(1)}) custom-call(s32[16]{0:T(128)S(1)} %dynamic_slice.11.slot_ref, bf16[4,32,2,32,512]{4,3,2,1,0:T(8,128)(2,1)} %get-tuple-element.9.grads_ref, f32[32,8,128]{2,1,0:T(8,128)S(1)} %get-tuple-element.10.mass_ref), custom_call_target="tpu_custom_call" | custom-call | tf_op jit(solution)/shard_map/pallas_call | solution.py:243
  479.7 0.0 copy-start.1
  479.7 1.9 copy-done.1
  481.6 0.2 reduce_sum.59
  481.8 0.5 multiply_convert_fusion
  482.3 4.8 copy.10
  (4 shorter events, 0.0 us)
Async XLA Ops:
  4.2 2.2 copy-start
  6.4 209.9 %copy-start.2 = (bf16[4,128,2048]{2,1,0:T(8,128)(2,1)S(1)}, bf16[4,128,2048]{2,1,0:T(8,128)(2,1)}, u32[]{:S(2)}) copy-start(bf16[4,128,2048]{2,1,0:T(8,128)(2,1)} %query_ref.1) | copy-start | bytes 6291460
  6.4 210.0 %copy-start.3 = (bf16[4,128,2048]{2,1,0:T(8,128)(2,1)S(1)}, bf16[4,128,2048]{2,1,0:T(8,128)(2,1)}, u32[]{:S(2)}) copy-start(bf16[4,128,2048]{2,1,0:T(8,128)(2,1)} %cot_ref.1) | copy-start | bytes 6291460
  479.7 1.9 copy-start.1

commit v2 on v1

--- a/solution.py
+++ b/solution.py
@@ -13,8 +13,8 @@
 ANS = 128
 SLOTS = 32
 LANES = 128
-CHUNKS = 4
-GROUP = 8
+CHUNKS = 8
+GROUP = 4
 MESH = pl.DeviceIdType.MESH
 VMEM_LIMIT = 48 * 1024 * 1024
 

time: 488 us -> 469 us (0.961)
  Pallas kernels: 473 us -> 453 us
    pallas_call x1, Pallas kernels: 55.4 us -> 44.6 us  [attend(): pl.pallas_call(attend_kernel, grid_spec=pltpu.PrefetchScalarGridSpec(num_...]
    pallas_call x1, Pallas kernels: 210 us -> 199 us  [dispatch(): pl.pallas_call(functools.partial(dispatch_kernel, n), out_shape=jax.Shape...]
where the time goes in v2:
time: 469 us; the launch traced here: 466 us
  Pallas kernels  453 us (97%)
  local copies, waits for them, and re-layouts  11.5 us (2%)
    pallas_call x1, Pallas kernels, collect(): pl.pallas_call(functools.partial(collect_kernel, n), out_shape=(jax.Shape...  208 us
    pallas_call x1, Pallas kernels, dispatch(): pl.pallas_call(functools.partial(dispatch_kernel, n), out_shape=jax.Shape...  199 us
    pallas_call x1, Pallas kernels, attend(): pl.pallas_call(attend_kernel, grid_spec=pltpu.PrefetchScalarGridSpec(num_...  44.6 us

profile of v2, /device:TPU:29, one launch (start us, length us, event | category | flops | bytes accessed | tf_op | source)
XLA Modules:
  0.0 466.4 jit_solution(15212669042215323053)
XLA Ops:
  0.6 0.8 dynamic_slice.11.slot_ref
  1.4 0.8 dynamic_slice.10
  2.2 0.8 dynamic_slice.9
  2.9 0.1 select_reduce_fusion.index_ref
  3.0 0.1 eq.20
  3.1 0.2 compare_reduce_fusion
  3.3 0.1 broadcast_in_dim.43
  3.4 0.2 fusion
  3.6 0.1 copy.8
  3.7 0.1 select_n.49
  3.8 0.2 convert_reduce_fusion.1
  4.0 0.2 convert_reduce_fusion.rank_ref
  4.2 0.0 copy-start
  4.2 2.2 copy-done
  6.4 0.0 copy-start.2
  6.4 0.0 copy-start.3
  6.4 199.5 %shard_map.76.recv_ref = bf16[8,32,2,32,256]{4,3,2,1,0:T(8,128)(2,1)} custom-call(s32[32]{0:T(128)S(1)} %select_reduce_fusion.index_ref, bf16[16,2,32,2048]{3,2,1,0:T(8,128)(2,1)S(1)} %copy-done), custom_call_target="tpu_custom_call" | custom-call | tf_op jit(solution)/shard_map/pallas_call | solution.py:101
  205.8 0.0 copy-done.2
  205.8 0.0 copy-done.3
  205.8 44.6 %shard_map.77 = (bf16[4,128,2048]{2,1,0:T(8,128)(2,1)}, bf16[8,32,2,32,256]{4,3,2,1,0:T(8,128)(2,1)}, f32[32,8,128]{2,1,0:T(8,128)S(1)}) custom-call(s32[32]{0:T(128)S(1)} %convert_reduce_fusion.rank_ref, s32[4]{0:T(128)S(1)} %get-tuple-element.14.start_ref, s32[4]{0:T(128)S(1)} %get-tuple-element.13.count_ref, bf16[4,128,2048]{2,1,0:T(8,128)(2,1)S(1)} %copy-done.2, ...), custom_call_target="tpu_custom_call" | custom-call | tf_op jit(solution)/shard_map/pallas_call | solution.py:395
  250.5 208.5 %shard_map.78 = (bf16[16,2,32,2048]{3,2,1,0:T(8,128)(2,1)S(1)}, f32[16,8,128]{2,1,0:T(8,128)S(1)}) custom-call(s32[16]{0:T(128)S(1)} %dynamic_slice.11.slot_ref, bf16[8,32,2,32,256]{4,3,2,1,0:T(8,128)(2,1)} %get-tuple-element.9.grads_ref, f32[32,8,128]{2,1,0:T(8,128)S(1)} %get-tuple-element.10.mass_ref), custom_call_target="tpu_custom_call" | custom-call | tf_op jit(solution)/shard_map/pallas_call | solution.py:243
  459.0 0.0 copy-start.1
  459.0 1.9 copy-done.1
  460.9 0.2 reduce_sum.59
  461.1 0.5 multiply_convert_fusion
  461.6 4.8 %copy.10 = bf16[16,2,32,2048]{3,2,1,0:T(8,128)(2,1)} copy(bf16[16,2,32,2048]{3,2,1,0:T(8,128)(2,1)} %copy-done.1) | data formatting | bytes 8388608
  (4 shorter events, 0.0 us)
Async XLA Ops:
  4.2 2.2 copy-start
  6.4 199.5 %copy-start.2 = (bf16[4,128,2048]{2,1,0:T(8,128)(2,1)S(1)}, bf16[4,128,2048]{2,1,0:T(8,128)(2,1)}, u32[]{:S(2)}) copy-start(bf16[4,128,2048]{2,1,0:T(8,128)(2,1)} %query_ref.1) | copy-start | bytes 6291460
  6.4 199.5 %copy-start.3 = (bf16[4,128,2048]{2,1,0:T(8,128)(2,1)S(1)}, bf16[4,128,2048]{2,1,0:T(8,128)(2,1)}, u32[]{:S(2)}) copy-start(bf16[4,128,2048]{2,1,0:T(8,128)(2,1)} %cot_ref.1) | copy-start | bytes 6291460
  459.0 1.9 copy-start.1

commit v3 on v2

--- a/solution.py
+++ b/solution.py
@@ -15,6 +15,7 @@
 LANES = 128
 CHUNKS = 8
 GROUP = 4
+AHEAD = 3
 MESH = pl.DeviceIdType.MESH
 VMEM_LIMIT = 48 * 1024 * 1024
 
@@ -170,7 +171,8 @@
         sends.append(copy)
     own_mass = pltpu.make_async_copy(mass_ref.at[my_rows], mass_back.at[my_rows], own_sem.at[CHUNKS])
     own_mass.start()
-    for c in range(CHUNKS):
+
+    def start_chunk(c):
         for d, peer in enumerate(peers, 1):
             copy = remote(
                 grads_ref.at[c, pl.ds(peer * per_pair, per_pair)],
@@ -185,6 +187,9 @@
         copy.start()
         locals_.append(copy)
 
+    for c in range(min(AHEAD, CHUNKS)):
+        start_chunk(c)
+
     def arrived(buffer, send_sem, recv_sem, d):
         source = lax.rem(me + n - d, n)
         landed = buffer.at[pl.ds(source * per_pair, per_pair)]
@@ -208,6 +213,8 @@
         locals_[c].wait()
         for d in range(1, n):
             arrived(back[c], z_send.at[c, d], z_recv.at[c, d], d)
+        if c + AHEAD < CHUNKS:
+            start_chunk(c + AHEAD)
 
         def pick(j, carry):
             dense[c, j] = back[c][slot_ref[j]]

time: 469 us -> 469 us (level)
  no operation moved by 1% of the time
where the time goes in v3:
time: 469 us; the launch traced here: 468 us
  Pallas kernels  454 us (97%)
  local copies, waits for them, and re-layouts  11.5 us (2%)
    pallas_call x1, Pallas kernels, collect(): pl.pallas_call(functools.partial(collect_kernel, n), out_shape=(jax.Shape...  210 us
    pallas_call x1, Pallas kernels, dispatch(): pl.pallas_call(functools.partial(dispatch_kernel, n), out_shape=jax.Shape...  199 us
    pallas_call x1, Pallas kernels, attend(): pl.pallas_call(attend_kernel, grid_spec=pltpu.PrefetchScalarGridSpec(num_...  44.6 us

profile of v3, /device:TPU:29, one launch (start us, length us, event | category | flops | bytes accessed | tf_op | source)
XLA Modules:
  0.0 468.1 jit_solution(10015117797303318251)
XLA Ops:
  0.6 0.8 dynamic_slice.11.slot_ref
  1.4 0.8 dynamic_slice.10
  2.2 0.8 dynamic_slice.9
  2.9 0.1 select_reduce_fusion.index_ref
  3.0 0.1 eq.20
  3.1 0.2 compare_reduce_fusion
  3.3 0.1 broadcast_in_dim.43
  3.4 0.2 fusion
  3.6 0.1 copy.8
  3.7 0.1 select_n.49
  3.8 0.2 convert_reduce_fusion.1
  4.0 0.2 convert_reduce_fusion.rank_ref
  4.2 0.0 copy-start
  4.2 2.2 copy-done
  6.4 0.0 copy-start.2
  6.4 0.0 copy-start.3
  6.4 199.5 %shard_map.76.recv_ref = bf16[8,32,2,32,256]{4,3,2,1,0:T(8,128)(2,1)} custom-call(s32[32]{0:T(128)S(1)} %select_reduce_fusion.index_ref, bf16[16,2,32,2048]{3,2,1,0:T(8,128)(2,1)S(1)} %copy-done), custom_call_target="tpu_custom_call" | custom-call | tf_op jit(solution)/shard_map/pallas_call | solution.py:102
  205.8 0.0 copy-done.2
  205.8 0.0 copy-done.3
  205.8 44.6 %shard_map.77 = (bf16[4,128,2048]{2,1,0:T(8,128)(2,1)}, bf16[8,32,2,32,256]{4,3,2,1,0:T(8,128)(2,1)}, f32[32,8,128]{2,1,0:T(8,128)S(1)}) custom-call(s32[32]{0:T(128)S(1)} %convert_reduce_fusion.rank_ref, s32[4]{0:T(128)S(1)} %get-tuple-element.14.start_ref, s32[4]{0:T(128)S(1)} %get-tuple-element.13.count_ref, bf16[4,128,2048]{2,1,0:T(8,128)(2,1)S(1)} %copy-done.2, ...), custom_call_target="tpu_custom_call" | custom-call | tf_op jit(solution)/shard_map/pallas_call | solution.py:402
  250.5 210.2 %shard_map.78 = (bf16[16,2,32,2048]{3,2,1,0:T(8,128)(2,1)S(1)}, f32[16,8,128]{2,1,0:T(8,128)S(1)}) custom-call(s32[16]{0:T(128)S(1)} %dynamic_slice.11.slot_ref, bf16[8,32,2,32,256]{4,3,2,1,0:T(8,128)(2,1)} %get-tuple-element.9.grads_ref, f32[32,8,128]{2,1,0:T(8,128)S(1)} %get-tuple-element.10.mass_ref), custom_call_target="tpu_custom_call" | custom-call | tf_op jit(solution)/shard_map/pallas_call | solution.py:250
  460.7 0.0 copy-start.1
  460.7 1.9 copy-done.1
  462.6 0.2 reduce_sum.59
  462.8 0.5 multiply_convert_fusion
  463.3 4.8 %copy.10 = bf16[16,2,32,2048]{3,2,1,0:T(8,128)(2,1)} copy(bf16[16,2,32,2048]{3,2,1,0:T(8,128)(2,1)} %copy-done.1) | data formatting | bytes 8388608
  (4 shorter events, 0.0 us)
Async XLA Ops:
  4.2 2.2 copy-start
  6.4 199.5 %copy-start.2 = (bf16[4,128,2048]{2,1,0:T(8,128)(2,1)S(1)}, bf16[4,128,2048]{2,1,0:T(8,128)(2,1)}, u32[]{:S(2)}) copy-start(bf16[4,128,2048]{2,1,0:T(8,128)(2,1)} %query_ref.1) | copy-start | bytes 6291460
  6.4 199.5 %copy-start.3 = (bf16[4,128,2048]{2,1,0:T(8,128)(2,1)S(1)}, bf16[4,128,2048]{2,1,0:T(8,128)(2,1)}, u32[]{:S(2)}) copy-start(bf16[4,128,2048]{2,1,0:T(8,128)(2,1)} %cot_ref.1) | copy-start | bytes 6291460
  460.7 1.9 copy-start.1
